TPU v7x, 256 devices: a whole 4x4x8 slice. The times are simulated.
256 devices in a mesh: prow: 32 (over x, y, core), pcol: 8 (over z).
Axes of the slice: x: 4, y: 4, z: 8, core: 2. Of those that a mesh axis runs over, the one named last changes fastest.
Arguments:
- right_sides: bfloat16 [4, 32, 256, 256], P(None, 'prow'), may hold values from -6 to 6
- lower_diag_inverse: bfloat16 [4, 32, 256, 256], P(None, 'prow'), may hold values from -1 to 2, as said below
- upper_diag_inverse: bfloat16 [4, 32, 256, 256], P(None, 'prow'), may hold values from -1 to 2, as said below
- lower_blocks: bfloat16 [6, 32, 32, 256, 256], P(None, 'prow', 'pcol'), may hold values from -0.375 to 0.375
- upper_blocks: bfloat16 [6, 32, 32, 256, 256], P(None, 'prow', 'pcol'), may hold values from -0.375 to 0.375
- block_mask: int32 [6, 32, 32], replicated, may hold values from 0 to 1, as said below
Outputs:
- solution: bfloat16 [4, 32, 256, 256], P(None, 'prow')
Inputs may be any that keep to these rules, and one draw needn't show every extreme that they name: Each supernode of a level has one parent on the next level; block_mask[p, i, j] is 1 exactly when supernode i of level h is the ancestor of supernode j of level g, else 0. Every supernode has exactly one ancestor on each higher level; supernodes differ in how many descendants they have. `lower_diag_inverse`: identity plus a dense part. `upper_diag_inverse`: identity plus a dense part.
All inputs are finite; a program needn't handle non-finite values.
Results may differ from a plain program's by a relative error of at most 0.03.
Values may be sent and summed in bfloat16 or wider, within the bound.
A program may use at most 64 MiB of HBM per device.

v0:
```python
import jax
import jax.numpy as jnp
from jax import lax
from jax.sharding import PartitionSpec as P


def per_device(
    right_sides, lower_diag_inverse, upper_diag_inverse, lower_blocks, upper_blocks, block_mask
):
    levels = right_sides.shape[0]
    row_count = lax.axis_size("prow")
    per_col = row_count // lax.axis_size("pcol")
    proc_row = lax.axis_index("prow")
    first_col = lax.axis_index("pcol") * per_col
    mask_f = block_mask.astype(jnp.float32)
    row_mask = lax.dynamic_slice_in_dim(
        lax.dynamic_index_in_dim(mask_f, proc_row, 1, keepdims=False), first_col, per_col, 1
    )
    col_mask = lax.dynamic_slice_in_dim(
        lax.dynamic_index_in_dim(mask_f, proc_row, 2, keepdims=False), first_col, per_col, 1
    )

    def spread_level(solved_piece):
        whole_level = lax.all_gather(solved_piece[None], "prow", axis=0, tiled=True)
        return lax.dynamic_slice_in_dim(whole_level, first_col, per_col, 0)

    def block_update(blocks, weights, columns):
        products = jnp.einsum("kab,kbr->kar", blocks, columns, preferred_element_type=jnp.float32)
        return jnp.einsum("k,kar->ar", weights, products)

    forward_entries = []
    forward_cols = []
    for tree_height in range(levels):
        source = right_sides[tree_height, 0].astype(jnp.float32)
        if tree_height > 0:
            pending_updates = jnp.zeros(source.shape, jnp.float32)
            for lower_neighbor in range(tree_height):
                pair_slot = tree_height * (tree_height - 1) // 2 + lower_neighbor
                pending_updates = pending_updates + block_update(
                    lower_blocks[pair_slot, 0], row_mask[pair_slot], forward_cols[lower_neighbor]
                )
            source = source - lax.psum(pending_updates, "pcol")
        residual_rows = source.astype(jnp.bfloat16)
        solved_rows = jnp.dot(
            lower_diag_inverse[tree_height, 0], residual_rows, preferred_element_type=jnp.float32
        ).astype(jnp.bfloat16)
        forward_entries.append(solved_rows)
        if tree_height < levels - 1:
            forward_cols.append(spread_level(solved_rows))
    backward_entries = [None] * levels
    backward_cols = [None] * levels
    for tree_height in range(levels - 1, -1, -1):
        source = forward_entries[tree_height].astype(jnp.float32)
        if tree_height < levels - 1:
            pending_updates = jnp.zeros(source.shape, jnp.float32)
            for upper_neighbor in range(tree_height + 1, levels):
                pair_slot = upper_neighbor * (upper_neighbor - 1) // 2 + tree_height
                pending_updates = pending_updates + block_update(
                    upper_blocks[pair_slot, 0], col_mask[pair_slot], backward_cols[upper_neighbor]
                )
            source = source - lax.psum(pending_updates, "pcol")
        residual_rows = source.astype(jnp.bfloat16)
        solved_rows = jnp.dot(
            upper_diag_inverse[tree_height, 0], residual_rows, preferred_element_type=jnp.float32
        ).astype(jnp.bfloat16)
        backward_entries[tree_height] = solved_rows
        if tree_height > 0:
            backward_cols[tree_height] = spread_level(solved_rows)
    return jnp.stack(backward_entries)[:, None]


def solution(mesh):
    in_specs = (
        P(None, "prow", None, None),
        P(None, "prow", None, None),
        P(None, "prow", None, None),
        P(None, "prow", "pcol", None, None),
        P(None, "prow", "pcol", None, None),
        P(),
    )
    out_specs = P(None, "prow", None, None)
    return jax.shard_map(
        per_device, mesh=mesh, in_specs=in_specs, out_specs=out_specs, check_vma=False
    )
```

profile of v0, /device:TPU:1, one launch (start us, length us, event | category | flops | bytes accessed | tf_op | source)
XLA Modules:
  0.0 814.8 jit_solution(4176500372926664494)
XLA Ops:
  6.5 1.9 convolution_convert_fusion.7
  8.5 0.9 convert_element_type.97
  9.4 55.8 %all-gather.13.cloned.1.call-done = bf16[8192,256]{1,0:T(8,128)(2,1)} async-done(((bf16[256,256]{1,0:T(8,128)(2,1)}), bf16[8192,256]{1,0:T(8,128)(2,1)}) %all-gather.13.cloned.1.call-update) | async-done | bytes 4194320 | tf_op jit(solution)/shard_map/all_gather | solution.py:24
  65.3 1.5 convolution_bitcast_fusion.11
  66.8 0.3 copy.8
  67.1 0.5 fusion.84
  67.6 0.7 copy.72
  68.4 67.1 %all-reduce.7.cloned.1.call-done = f32[256,256]{1,0:T(8,128)} async-done(((f32[256,256]{1,0:T(8,128)}), f32[256,256]{1,0:T(8,128)}) %all-reduce.7.cloned.1.call-update) | async-done | bytes 262160 | tf_op jit(solution)/shard_map/psum | solution.py:42
  135.5 1.8 fusion.6
  137.4 1.5 convolution_bitcast_fusion.10
  138.9 0.3 copy.10
  139.2 0.5 fusion.90
  139.7 56.2 %all-gather.15.cloned.1.call-done = bf16[8192,256]{0,1:T(8,128)(2,1)} async-done(((bf16[256,256]{0,1:T(8,128)(2,1)}), bf16[8192,256]{0,1:T(8,128)(2,1)}) %all-gather.15.cloned.1.call-update) | async-done | bytes 4194320 | tf_op jit(solution)/shard_map/all_gather | solution.py:24
  195.9 3.6 copy.40
  199.5 0.3 constant_dynamic-slice_fusion.5
  199.8 1.4 convolution_bitcast_fusion.9
  201.1 0.3 copy.13
  201.4 0.5 fusion.89
  201.9 0.7 bitcast_add_fusion.4
  202.8 67.2 %all-reduce.9.cloned.1.call-done = f32[256,256]{1,0:T(8,128)} async-done(((f32[256,256]{1,0:T(8,128)}), f32[256,256]{1,0:T(8,128)}) %all-reduce.9.cloned.1.call-update) | async-done | bytes 262160 | tf_op jit(solution)/shard_map/psum | solution.py:42
  270.0 1.8 fusion.7
  271.9 1.5 convolution_bitcast_fusion.8
  273.4 0.3 copy.15
  273.7 0.5 fusion.88
  274.2 1.4 convolution_bitcast_fusion.7
  275.6 0.3 copy.17
  275.9 0.5 fusion.87
  276.4 53.5 %all-gather.17.cloned.1.call-done = bf16[8192,256]{0,1:T(8,128)(2,1)} async-done(((bf16[256,256]{0,1:T(8,128)(2,1)}), bf16[8192,256]{0,1:T(8,128)(2,1)}) %all-gather.17.cloned.1.call-update) | async-done | bytes 4194320 | tf_op jit(solution)/shard_map/all_gather | solution.py:24
  329.9 3.6 copy.41
  333.8 1.4 convolution_bitcast_fusion.6
  335.2 0.3 copy.20
  335.5 0.5 fusion.86
  336.0 0.8 bitcast_add_fusion.2
  336.8 67.2 %all-reduce.11.cloned.1.call-done = f32[256,256]{1,0:T(8,128)} async-done(((f32[256,256]{1,0:T(8,128)}), f32[256,256]{1,0:T(8,128)}) %all-reduce.11.cloned.1.call-update) | async-done | bytes 262160 | tf_op jit(solution)/shard_map/psum | solution.py:42
  404.1 2.0 convolution_convert_fusion.3
  406.5 57.9 %all-gather.19.cloned.1.call-done = bf16[8192,256]{0,1:T(8,128)(2,1)} async-done(((bf16[256,256]{0,1:T(8,128)(2,1)}), bf16[8192,256]{0,1:T(8,128)(2,1)}) %all-gather.19.cloned.1.call-update) | async-done | bytes 4194320 | tf_op jit(solution)/shard_map/all_gather | solution.py:24
  464.5 3.6 copy.42
  468.4 2.1 fusion.3
  470.5 67.2 %all-reduce.13.cloned.1.call-done = f32[256,256]{0,1:T(8,128)} async-done(((f32[256,256]{0,1:T(8,128)}), f32[256,256]{0,1:T(8,128)}) %all-reduce.13.cloned.1.call-update) | async-done | bytes 262160 | tf_op jit(solution)/shard_map/psum | solution.py:61
  537.7 1.8 convolution_convert_fusion.2
  539.6 1.4 fusion.5
  541.0 56.8 %all-gather.21.cloned.1.call-done = bf16[8192,256]{0,1:T(8,128)(2,1)} async-done(((bf16[256,256]{0,1:T(8,128)(2,1)}), bf16[8192,256]{0,1:T(8,128)(2,1)}) %all-gather.21.cloned.1.call-update) | async-done | bytes 4194320 | tf_op jit(solution)/shard_map/all_gather | solution.py:24
  597.8 3.6 copy.43
  601.4 0.3 constant_dynamic-slice_fusion.2
  601.7 1.4 fusion.4
  603.1 0.7 add.57
  603.9 67.2 %all-reduce.15.cloned.1.call-done = f32[256,256]{0,1:T(8,128)} async-done(((f32[256,256]{0,1:T(8,128)}), f32[256,256]{0,1:T(8,128)}) %all-reduce.15.cloned.1.call-update) | async-done | bytes 262160 | tf_op jit(solution)/shard_map/psum | solution.py:61
  671.1 1.8 convolution_convert_fusion.1
  673.0 1.4 convolution_bitcast_fusion
  674.4 0.3 copy.38
  674.7 0.4 fusion.91
  675.1 1.4 convolution_bitcast_fusion.1
  676.5 0.3 copy.36
  676.8 0.4 fusion.93
  677.3 54.3 %all-gather.23.cloned.1.call-done = bf16[8192,256]{0,1:T(8,128)(2,1)} async-done(((bf16[256,256]{0,1:T(8,128)(2,1)}), bf16[8192,256]{0,1:T(8,128)(2,1)}) %all-gather.23.cloned.1.call-update) | async-done | bytes 4194320 | tf_op jit(solution)/shard_map/all_gather | solution.py:24
  731.6 3.6 copy.44
  735.2 0.3 constant_dynamic-slice_fusion.1
  735.5 1.4 convolution_bitcast_fusion.2
  736.9 0.3 copy.34
  737.2 0.4 fusion.95
  737.6 0.8 bitcast_add_fusion
  738.4 67.3 %all-reduce.17.cloned.1.call-done = f32[256,256]{1,0:T(8,128)} async-done(((f32[256,256]{1,0:T(8,128)}), f32[256,256]{1,0:T(8,128)}) %all-reduce.17.cloned.1.call-update) | async-done | bytes 262160 | tf_op jit(solution)/shard_map/psum | solution.py:61
  805.6 1.2 fusion.8
  806.9 1.0 copy.7
  (46 shorter events, 1.8 us)
Async XLA Ops:
  6.5 128.9 %copy-start.7 = (bf16[4,1,256,256]{3,2,1,0:T(8,128)(2,1)S(1)}, bf16[4,1,256,256]{3,2,1,0:T(8,128)(2,1)}, u32[]{:S(2)}) copy-start(bf16[4,1,256,256]{3,2,1,0:T(8,128)(2,1)} %param.7) | copy-start | bytes 1572868
  6.5 128.9 %copy-start.6 = (bf16[4,1,256,256]{3,2,1,0:T(8,128)(2,1)S(1)}, bf16[4,1,256,256]{3,2,1,0:T(8,128)(2,1)}, u32[]{:S(2)}) copy-start(bf16[4,1,256,256]{3,2,1,0:T(8,128)(2,1)} %param.6) | copy-start | bytes 1572868
  6.5 58.7 %all-gather.13.cloned.1.call-start = ((), (), s32[]{:S(2)}) async-start(), calls=%async_computation.6 | async-start | bytes 4325376 | tf_op jit(solution)/shard_map/all_gather | solution.py:24
  8.5 127.0 %all-reduce.7.cloned.1.call-start = ((), (), s32[]{:S(2)}) async-start(), calls=%async_computation | async-start | bytes 524288 | tf_op jit(solution)/shard_map/psum | solution.py:42
  68.3 127.6 %all-gather.15.cloned.1.call-start = ((), (), s32[]{:S(2)}) async-start(), calls=%async_computation.7 | async-start | bytes 4325376 | tf_op jit(solution)/shard_map/all_gather | solution.py:24
  137.3 132.6 %all-reduce.9.cloned.1.call-start = ((), (), s32[]{:S(2)}) async-start(), calls=%async_computation.1 | async-start | bytes 524288 | tf_op jit(solution)/shard_map/psum | solution.py:42
  202.7 127.2 %all-gather.17.cloned.1.call-start = ((), (), s32[]{:S(2)}) async-start(), calls=%async_computation.8 | async-start | bytes 4325376 | tf_op jit(solution)/shard_map/all_gather | solution.py:24
  271.8 132.2 %all-reduce.11.cloned.1.call-start = ((), (), s32[]{:S(2)}) async-start(), calls=%async_computation.2 | async-start | bytes 524288 | tf_op jit(solution)/shard_map/psum | solution.py:42
  333.5 70.6 %copy-start.8 = (bf16[4,1,256,256]{3,2,1,0:T(8,128)(2,1)S(1)}, bf16[4,1,256,256]{3,2,1,0:T(8,128)(2,1)}, u32[]{:S(2)}) copy-start(bf16[4,1,256,256]{3,2,1,0:T(8,128)(2,1)} %param.8) | copy-start | bytes 1572868
  336.8 127.7 %all-gather.19.cloned.1.call-start = ((), (), s32[]{:S(2)}) async-start(), calls=%async_computation.9 | async-start | bytes 4325376 | tf_op jit(solution)/shard_map/all_gather | solution.py:24
  406.0 131.6 %all-reduce.13.cloned.1.call-start = ((), (), s32[]{:S(2)}) async-start(), calls=%async_computation.3 | async-start | bytes 524288 | tf_op jit(solution)/shard_map/psum | solution.py:61
  468.0 69.6 %copy-start.2 = (bf16[256,256]{0,1:T(8,128)(2,1)S(1)}, bf16[256,256]{0,1:T(8,128)(2,1)}, u32[]{:S(2)}) copy-start(bf16[256,256]{0,1:T(8,128)(2,1)} %fusion.7) | copy-start | bytes 393220
  470.5 127.3 %all-gather.21.cloned.1.call-start = ((), (), s32[]{:S(2)}) async-start(), calls=%async_computation.10 | async-start | bytes 4325376 | tf_op jit(solution)/shard_map/all_gather | solution.py:24
  539.5 131.6 %all-reduce.15.cloned.1.call-start = ((), (), s32[]{:S(2)}) async-start(), calls=%async_computation.4 | async-start | bytes 524288 | tf_op jit(solution)/shard_map/psum | solution.py:61
  601.4 69.8 %copy-start.1 = (bf16[256,256]{0,1:T(8,128)(2,1)S(1)}, bf16[256,256]{0,1:T(8,128)(2,1)}, u32[]{:S(2)}) copy-start(bf16[256,256]{0,1:T(8,128)(2,1)} %fusion.6) | copy-start | bytes 393220
  603.9 127.7 %all-gather.23.cloned.1.call-start = ((), (), s32[]{:S(2)}) async-start(), calls=%async_computation.11 | async-start | bytes 4325376 | tf_op jit(solution)/shard_map/all_gather | solution.py:24
  673.0 132.6 %all-reduce.17.cloned.1.call-start = ((), (), s32[]{:S(2)}) async-start(), calls=%async_computation.5 | async-start | bytes 524288 | tf_op jit(solution)/shard_map/psum | solution.py:61
  735.1 70.5 %copy-start = (bf16[256,256]{1,0:T(8,128)(2,1)S(1)}, bf16[256,256]{1,0:T(8,128)(2,1)}, u32[]{:S(2)}) copy-start(bf16[256,256]{1,0:T(8,128)(2,1)} %convolution_convert_fusion.7) | copy-start | bytes 393220
  735.1 71.7 %copy-start.3 = (bf16[256,256]{1,0:T(8,128)(2,1)S(1)}, bf16[256,256]{1,0:T(8,128)(2,1)}, u32[]{:S(2)}) copy-start(bf16[256,256]{1,0:T(8,128)(2,1)} %convolution_convert_fusion.2) | copy-start | bytes 393220
  735.2 71.7 %copy-start.4 = (bf16[256,256]{1,0:T(8,128)(2,1)S(1)}, bf16[256,256]{1,0:T(8,128)(2,1)}, u32[]{:S(2)}) copy-start(bf16[256,256]{1,0:T(8,128)(2,1)} %convolution_convert_fusion.1) | copy-start | bytes 393220
  735.2 71.7 %copy-start.5 = (bf16[256,256]{1,0:T(8,128)(2,1)S(1)}, bf16[256,256]{1,0:T(8,128)(2,1)}, u32[]{:S(2)}) copy-start(bf16[256,256]{1,0:T(8,128)(2,1)} %convolution_convert_fusion.3) | copy-start | bytes 393220
Sparse Core Ops, SparseCore 0:
  9.9 55.2 all-gather.12
  68.5 66.9 all-reduce.6
  138.2 57.6 all-gather.14
  202.8 67.0 all-reduce.8
  272.3 57.6 all-gather.16
  336.9 67.1 all-reduce.10
  406.8 57.6 all-gather.18
  470.6 67.0 all-reduce.12
  540.2 57.6 all-gather.20
  604.0 67.1 all-reduce.14
  673.9 57.6 all-gather.22
  738.5 67.0 all-reduce.16
where the time goes:
time: 819 us; the launch traced here: 815 us
  waiting for transfers between devices  738 us (90%)
  matrix products  34.4 us (4%)
  local copies, waits for them, and re-layouts  23.9 us (3%)
  between operations  14 us (2%)
    psum x6, waiting for transfers between devices, per_device(): source = source - lax.psum(pending_updates, 'pcol')  403 us
    all_gather x6, waiting for transfers between devices, spread_level(): whole_level = lax.all_gather(solved_piece[None], 'prow', axis=0, tiled=True)  335 us
    dot_general x12, matrix products, block_update(): jnp.einsum('kab,kbr->kar', blocks, columns, preferred_element_type=jnp.fl...  17.8 us
    unnamed x23, local copies, waits for them, and re-layouts  17.8 us
  transfers between devices with their start and end apart: 12, of which 12 were waited for; matrix products, arithmetic and copies ran while one was open for 2% of the time, Pallas kernels for 0%

commit v1 on v0

v1 whole, which is shorter than its diff:
```python
import functools

import jax
import jax.numpy as jnp
from jax import lax
from jax.experimental import pallas as pl
from jax.experimental.pallas import tpu as pltpu
from jax.sharding import PartitionSpec as P

MESH = pl.DeviceIdType.MESH
F32 = jnp.float32
BF16 = jnp.bfloat16
B = 256
LEV = 4
NPAIR = 6
CHIPS = 16
NZ = 8
W = 16
FIRST = (0, 1, 3)
MOVED = (2, 5, 4)
UORD = (5, 2, 4, 0, 1, 3)
UROW = (2, 1, 1, 0, 0, 0)
ROW_OF = (1, 2, 2, 3, 3, 3)
UGROUPS = ((0, 1), (1, 3), (3, 6))


def dot_nt(a, b):
    return lax.dot_general(a, b, (((1,), (1,)), ((), ())), preferred_element_type=F32)


def kernel(
    rhs_hbm, linv_hbm, uinv_hbm, lower_hbm, upper_hbm, mask,
    out_hbm,
    rhs, linv, uinv, lower, upper,
    g_all, g_home, home, x0, first_m, part, zsum,
    mov, mov_sib, comb, rs_buf, piece, lact,
    ucand, ur_buf, upiece, uact0, uact1, uact2,
    fv, u_src, u21, u32, u31,
    sol, s3, s2, s1, out_buf, out_t,
    load_sem, send_sem, recv_sem,
):
    row = lax.axis_index("prow")
    z = lax.axis_index("pcol")
    q = row // 2
    core = row % 2
    other = 1 - core

    def dev(chip, c, zz):
        return (chip * 2 + c, zz)

    sibling = dev(q, other, z)

    loads = {}
    n_load = [0]

    def load(name, src, dst):
        copy = pltpu.make_async_copy(src, dst, load_sem.at[n_load[0]])
        n_load[0] += 1
        copy.start()
        loads[name] = copy

    load("linv", linv_hbm.at[:, 0], linv)
    load("rhs", rhs_hbm.at[:, 0], rhs)
    for p in (2, 0, 5, 4, 1, 3):
        load(("l", p), lower_hbm.at[p, 0], lower.at[p])
    load("uinv", uinv_hbm.at[:, 0], uinv.at[core])
    load("upper", upper_hbm.at[:, 0], upper)

    plane = q // 2
    x, y, qb = q // 4, q % 4, q % 2
    turn = (z - plane + 9) % 8
    flag = 1 - turn // 4
    hx = (x + 3 + 2 * (1 - flag) - turn + 8) % 4
    hy = (y + flag * (2 * qb - 1) + 4) % 4
    home_chip = hx * 4 + hy
    dx = (x - z // 2 + 4) % 4
    dy = (y - 2 * (z % 2) + 4) % 4
    src_qb = ((dy + 1) % 4) // 2
    src_v = 1 - dy // 2
    src_turn = 4 * src_v + (3 + 2 * src_v - dx + 4) % 4
    src_z = (src_turn + 7 + z) % 8
    src_chip = 2 * z + src_qb
    slot = src_qb * 8 + src_z

    barrier = pltpu.get_barrier_semaphore()

    def greet(device):
        pl.semaphore_signal(barrier, inc=1, device_id=device, device_id_type=MESH)

    def greet_plane(d, _):
        greet(dev((q + d) % CHIPS, core, z))
        return 0

    def greet_z(d, _):
        greet(dev(q, core, (z + d) % NZ))
        return 0

    def greet_cross(d, _):
        greet(dev(q, other, (z + d) % NZ))
        return 0

    move_src = (q // 2, q % 2)

    def greet_move(d, _):
        greet(dev((q + d) % CHIPS, move_src[1], move_src[0]))
        return 0

    own_move = jnp.logical_and(z == q // 2, core == q % 2)
    greet(dev(src_chip, core, src_z))
    greet(dev(src_chip, other, src_z))
    lax.fori_loop(0, NZ, greet_cross, 0)
    lax.fori_loop(1, CHIPS, greet_plane, 0)
    lax.fori_loop(1, NZ, greet_z, 0)
    lax.fori_loop(1, CHIPS, greet_move, 0)

    @pl.when(jnp.logical_not(own_move))
    def _():
        greet(dev(q, move_src[1], move_src[0]))

    sent = []

    def remote(src, dst, sem, device):
        pltpu.make_async_remote_copy(
            src_ref=src, dst_ref=dst, send_sem=send_sem.at[sem], recv_sem=recv_sem.at[sem],
            device_id=device, device_id_type=MESH,
        ).start()

    def wait_recv(sem, ref):
        pltpu.make_async_copy(ref, ref, recv_sem.at[sem]).wait()

    sems = {}

    def new_sem(name):
        sems[name] = len(sems)
        return sems[name]

    def to_sibling(name, src, dst):
        sem = new_sem(name)
        remote(src, dst, sem, sibling)
        sent.append((sem, src))

    def plane_gather(name, src, buf, at):
        sem = new_sem(name)

        def body(d, _):
            remote(src, buf.at[at], sem, dev((q + d) % CHIPS, core, z))
            return 0

        lax.fori_loop(1, CHIPS, body, 0)
        buf[at] = src[...]
        sent.append((sem, buf.at[pl.ds(0, 15)] if len(buf.shape) == 4 else buf.at[pl.ds(0, 30)]))

    def plane_wait(name, buf):
        wait_recv(sems[name], buf.at[pl.ds(0, 15)] if len(buf.shape) == 4 else buf.at[pl.ds(0, 30)])

    def z_exchange(name, src_of, buf, at):
        sem = new_sem(name)

        def body(d, _):
            zz = (z + d) % NZ
            remote(src_of(zz), buf.at[at], sem, dev(q, core, zz))
            return 0

        lax.fori_loop(1, NZ, body, 0)
        sent.append((sem, buf.at[pl.ds(0, 7)]))

    loads["linv"].wait()
    loads["rhs"].wait()

    def make_g(h):
        g_all[h] = jnp.dot(linv[h], rhs[h], preferred_element_type=F32).T.astype(BF16)

    def make_m(p, dst, first):
        if first:
            loads[("l", p)].wait()
        for k in range(4):
            weight = mask[p, row, 4 * z + k].astype(F32)
            dst[k] = (jnp.dot(linv[ROW_OF[p]], lower[p, k], preferred_element_type=F32) * weight).astype(BF16)

    make_g(0)
    make_m(2, mov.at[0], True)
    make_m(0, first_m.at[core, 0], True)
    pl.semaphore_wait(barrier, 48 - own_move.astype(jnp.int32))

    sem = new_sem("home")
    mine = pl.ds(pl.multiple_of(core * 128 + z * W, W), W)
    yours = pl.ds(pl.multiple_of(other * 128 + z * W, W), W)
    remote(g_all.at[0, mine], home.at[core], sem, dev(home_chip, core, plane))
    remote(g_all.at[0, yours], home.at[core], sem, dev(home_chip, other, plane))
    sent.append((sem, home))

    def move_to_sibling(i):
        to_sibling(("mov", i), mov.at[i, pl.ds(2 * other, 2)], mov_sib.at[i])

    move_to_sibling(0)
    to_sibling(("m", 0), first_m.at[core, 0], first_m.at[core, 0])

    for h in range(1, LEV):
        make_g(h)
    to_sibling("g", g_all.at[:, yours], g_home.at[core])
    g_home[core] = g_all[:, mine]

    for i in (1, 2):
        make_m(MOVED[i], mov.at[i], True)
        move_to_sibling(i)

    def combine(i):
        wait_recv(sems[("mov", i)], mov_sib.at[i])
        for e in range(2):
            comb[i, e] = mov[i, 2 * core + e] + mov_sib[i, e]
        sem = new_sem(("rs", i))

        def body(d, _):
            chip = (q + d) % CHIPS
            rows = pl.ds(pl.multiple_of(chip * W, W), W)
            remote(comb.at[i, :, rows], rs_buf.at[i, q], sem, dev(chip, core, z))
            return 0

        lax.fori_loop(1, CHIPS, body, 0)
        rs_buf[i, q] = comb[i, :, pl.ds(pl.multiple_of(q * W, W), W)]
        sent.append((sem, rs_buf.at[i, pl.ds(0, 15)]))

    combine(0)

    wait_recv(sems["home"], home)
    plane_gather("x0", home, x0, slot)

    for i in (1, 2):
        make_m(FIRST[i], first_m.at[core, i], True)
        to_sibling(("m", i), first_m.at[core, i], first_m.at[core, i])
    combine(1)
    combine(2)

    def spread(i):
        wait_recv(sems[("rs", i)], rs_buf.at[i, pl.ds(0, 15)])
        total = rs_buf[i, 0].astype(F32)
        for s in range(1, CHIPS):
            total = total + rs_buf[i, s].astype(F32)
        piece[i] = total.astype(BF16)
        sem = new_sem(("lact", i))
        chip = 2 * z + core

        def body(t, _):
            remote(piece.at[i], lact.at[i, q], sem, dev(chip, (core + t) % 2, (z + t // 2) % NZ))
            return 0

        lax.fori_loop(1, 16, body, 0)

        @pl.when(own_move)
        def _():
            lact[i, q] = piece[i]

        @pl.when(jnp.logical_not(own_move))
        def _():
            remote(piece.at[i], lact.at[i, q], sem, dev(chip, core, z))

        return sem

    def wait_moved(sem_ref, i):
        @pl.when(own_move)
        def _():
            ref = lact.at[i, pl.ds(0, 15)]
            pltpu.make_async_copy(ref, ref, sem_ref).wait()

        @pl.when(jnp.logical_not(own_move))
        def _():
            ref = lact.at[i]
            pltpu.make_async_copy(ref, ref, sem_ref).wait()

    spread_sems = [spread(0)]

    loads["uinv"].wait()
    to_sibling("uinv", uinv.at[core], uinv.at[core])
    loads["upper"].wait()
    for n, p in enumerate(UORD):
        found = jnp.int32(0)
        at = jnp.int32(0)
        for k in range(4):
            bit = mask[p, 4 * z + k, row]
            found = found + bit
            at = at + k * bit
        block = jnp.dot(uinv[core, UROW[n]], upper[p, at], preferred_element_type=F32) * found.astype(F32)
        ucand[n] = block.astype(BF16)

    plane_wait("x0", x0)

    def products(i):
        wait_recv(sems[("m", i)], first_m.at[0, 0])
        for e in range(2):
            total = None
            for k in range(4):
                cols = x0[8 * (k // 2):8 * (k // 2) + 8, k % 2].reshape(128, B)
                term = dot_nt(cols, first_m[e, i, k])
                total = term if total is None else total + term
            part[i, :, e] = total.astype(BF16).reshape(NZ, W, B)
        z_exchange(("z", i), lambda zz: part.at[i, zz], zsum.at[i], z)
        zsum[i, z] = part[i, z]

    products(0)
    products(1)
    products(2)
    spread_sems.append(spread(1))
    spread_sems.append(spread(2))

    sem = new_sem("ur")

    def ur_body(d, _):
        zz = (z + d) % NZ
        rows = pl.ds(pl.multiple_of(zz * 32, 32), 32)
        remote(ucand.at[:, rows], ur_buf.at[z], sem, dev(q, core, zz))
        return 0

    lax.fori_loop(1, NZ, ur_body, 0)
    ur_buf[z] = ucand[:, pl.ds(pl.multiple_of(z * 32, 32), 32)]
    sent.append((sem, ur_buf.at[pl.ds(0, 7)]))

    def z_total(i):
        wait_recv(sems[("z", i)], zsum.at[i, pl.ds(0, 7)])
        total = zsum[i, 0].astype(F32)
        for s in range(1, NZ):
            total = total + zsum[i, s].astype(F32)
        return total

    def pushed(i, buf, p):
        def body(t, carry):
            for j in [t * 8 + u for u in range(8)]:
                val = buf[j].astype(F32)
                carry = tuple(carry[e] + val * mask[p, 2 * q + e, j].astype(F32) for e in range(2))
            return carry

        zero = jnp.zeros((W, B), F32)
        return lax.fori_loop(0, 4, body, (zero, zero))

    def push(name, level, i, slot_, buf):
        for e in range(2):
            block = lact[i, :, e].reshape(B, B)
            u_src[slot_, e] = dot_nt(fv[level, e], block).astype(BF16)
        plane_gather(name, u_src.at[slot_], buf, pl.ds(2 * q, 2))

    wait_recv(sems["g"], g_home.at[0])
    base = z_total(0)
    for e in range(2):
        fv[0, e] = g_home[e, 0]
        fv[1, e] = (g_home[e, 1].astype(F32) - base[e]).astype(BF16)
    wait_moved(recv_sem.at[spread_sems[0]], 0)
    push("u21", 1, 0, 0, u21)

    wait_moved(recv_sem.at[spread_sems[2]], 2)
    push("u31", 1, 2, 1, u31)

    wait_recv(sems["ur"], ur_buf.at[pl.ds(0, 7)])
    total = ur_buf[0].astype(F32)
    for s in range(1, NZ):
        total = total + ur_buf[s].astype(F32)
    upiece[...] = total.astype(BF16)
    uacts = (uact0, uact1, uact2)

    def spread_upper(n):
        lo, hi = UGROUPS[n]
        uact = uacts[n]
        sem = new_sem(("ua", n))

        def body(d, _):
            remote(upiece.at[pl.ds(lo, hi - lo)], uact.at[core, z], sem, dev(q, core, (z + d) % NZ))
            return 0

        lax.fori_loop(1, NZ, body, 0)
        uact[core, z] = upiece[lo:hi]
        sent.append((sem, uact.at[0, pl.ds(0, 7)]))

    def pass_upper(n):
        wait_recv(sems[("ua", n)], uacts[n].at[0, pl.ds(0, 7)])
        to_sibling(("us", n), uacts[n].at[core], uacts[n].at[core])

    def upper_ready(n):
        wait_recv(sems[("us", n)], uacts[n].at[0])

    for n in range(3):
        spread_upper(n)

    plane_wait("u21", u21)
    low, high = pushed(0, u21, 2)
    base = g_home[:, 2].astype(F32) - z_total(1)
    fv[2, 0] = (base[0] - low).astype(BF16)
    fv[2, 1] = (base[1] - high).astype(BF16)
    wait_moved(recv_sem.at[spread_sems[1]], 1)
    push("u32", 2, 1, 2, u32)

    base = g_home[:, 3].astype(F32) - z_total(2)
    plane_wait("u31", u31)
    low1, high1 = pushed(1, u31, 4)
    pass_upper(0)
    plane_wait("u32", u32)
    low, high = pushed(1, u32, 5)
    fv[3, 0] = (base[0] - low1 - low).astype(BF16)
    fv[3, 1] = (base[1] - high1 - high).astype(BF16)

    wait_recv(sems["uinv"], uinv.at[0])

    def own_term(level, e):
        return dot_nt(fv[level, e], uinv[e, level])

    def above(buf, n):
        group = sum(n >= lo for lo, _ in UGROUPS) - 1
        p = UORD[n]

        def body(t, chosen):
            for j in [t * 8 + u for u in range(8)]:
                val = buf[j].astype(F32)
                chosen = tuple(jnp.where(mask[p, j, 2 * q + e] == 1, val, chosen[e]) for e in range(2))
            return chosen

        zero = jnp.zeros((W, B), F32)
        chosen = lax.fori_loop(0, 4, body, (zero, zero))
        blocks = [uacts[group][e, :, n - UGROUPS[group][0]].reshape(B, B) for e in range(2)]
        return [dot_nt(chosen[e].astype(BF16), blocks[e]) for e in range(2)]

    def publish(level, buf):
        if buf is not None:
            plane_gather(("s", level), sol.at[level], buf, pl.ds(2 * q, 2))
        sem = new_sem(("out", level))
        at = core * 8 + z

        def body(d, _):
            remote(sol.at[level, core], out_buf.at[level, at], sem, dev(q, core, (z + d) % NZ))
            return 0

        def cross(d, _):
            remote(sol.at[level, other], out_buf.at[level, at], sem, dev(q, other, (z + d) % NZ))
            return 0

        lax.fori_loop(1, NZ, body, 0)
        lax.fori_loop(0, NZ, cross, 0)
        out_buf[level, at] = sol[level, core]
        sent.append((sem, out_buf.at[level, pl.ds(0, 15)]))

    stores = []

    def finish(level):
        wait_recv(sems[("out", level)], out_buf.at[level, pl.ds(0, 15)])
        out_t[level] = out_buf[level].reshape(B, B).astype(F32).T.astype(BF16)
        copy = pltpu.make_async_copy(out_t.at[level], out_hbm.at[level, 0], load_sem.at[n_load[0]])
        n_load[0] += 1
        copy.start()
        stores.append(copy)

    for e in range(2):
        sol[3, e] = own_term(3, e).astype(BF16)
    publish(3, s3)
    pass_upper(1)
    rest = [own_term(2, e) for e in range(2)]
    upper_ready(0)
    plane_wait(("s", 3), s3)
    terms = above(s3, 0)
    for e in range(2):
        sol[2, e] = (rest[e] - terms[e]).astype(BF16)
    publish(2, s2)
    pass_upper(2)
    upper_ready(1)
    terms = above(s3, 2)
    rest = [own_term(1, e) - terms[e] for e in range(2)]
    finish(3)
    plane_wait(("s", 2), s2)
    terms = above(s2, 1)
    for e in range(2):
        sol[1, e] = (rest[e] - terms[e]).astype(BF16)
    publish(1, s1)
    upper_ready(2)
    terms = above(s3, 5)
    more = above(s2, 4)
    rest = [own_term(0, e) - terms[e] - more[e] for e in range(2)]
    finish(2)
    plane_wait(("s", 1), s1)
    terms = above(s1, 3)
    for e in range(2):
        sol[0, e] = (rest[e] - terms[e]).astype(BF16)
    publish(0, None)
    finish(1)

    for sem, ref in sent:
        pltpu.make_async_copy(ref, ref, send_sem.at[sem]).wait()

    for i in range(3):
        wait_moved(send_sem.at[spread_sems[i]], i)

    finish(0)
    for copy in stores:
        copy.wait()


def per_device(right_sides, lower_diag_inverse, upper_diag_inverse, lower_blocks, upper_blocks, block_mask):
    def vmem(*shape):
        return pltpu.VMEM(shape, BF16)

    anywhere = pl.BlockSpec(memory_space=pl.ANY)
    return pl.pallas_call(
        kernel,
        out_shape=jax.ShapeDtypeStruct(right_sides.shape, BF16),
        in_specs=[anywhere] * 5 + [pl.BlockSpec(memory_space=pltpu.SMEM)],
        out_specs=anywhere,
        scratch_shapes=[
            vmem(LEV, B, B),
            vmem(LEV, B, B),
            vmem(2, LEV, B, B),
            vmem(NPAIR, 4, B, B),
            vmem(NPAIR, 4, B, B),
            vmem(LEV, B, B),
            vmem(2, LEV, W, B),
            vmem(2, W, B),
            vmem(CHIPS, 2, W, B),
            vmem(2, 3, 4, B, B),
            vmem(3, NZ, 2, W, B),
            vmem(3, NZ, 2, W, B),
            vmem(3, 4, B, B),
            vmem(3, 2, B, B),
            vmem(3, 2, B, B),
            vmem(3, CHIPS, 2, W, B),
            vmem(3, 2, W, B),
            vmem(3, CHIPS, 2, W, B),
            vmem(NPAIR, B, B),
            vmem(NZ, NPAIR, 32, B),
            vmem(NPAIR, 32, B),
            vmem(2, NZ, 1, 32, B),
            vmem(2, NZ, 2, 32, B),
            vmem(2, NZ, 3, 32, B),
            vmem(LEV, 2, W, B),
            vmem(3, 2, W, B),
            vmem(32, W, B),
            vmem(32, W, B),
            vmem(32, W, B),
            vmem(LEV, 2, W, B),
            vmem(32, W, B),
            vmem(32, W, B),
            vmem(32, W, B),
            vmem(LEV, 16, W, B),
            vmem(LEV, B, B),
            pltpu.SemaphoreType.DMA((16,)),
            pltpu.SemaphoreType.DMA((48,)),
            pltpu.SemaphoreType.DMA((48,)),
        ],
        compiler_params=pltpu.CompilerParams(
            collective_id=0, has_side_effects=True, vmem_limit_bytes=48 * 2**20
        ),
        name="tree_solve",
    )(right_sides, lower_diag_inverse, upper_diag_inverse, lower_blocks, upper_blocks, block_mask)


def solution(mesh):
    in_specs = (
        P(None, "prow", None, None),
        P(None, "prow", None, None),
        P(None, "prow", None, None),
        P(None, "prow", "pcol", None, None),
        P(None, "prow", "pcol", None, None),
        P(),
    )
    return jax.shard_map(
        per_device, mesh=mesh, in_specs=in_specs, out_specs=P(None, "prow", None, None), check_vma=False
    )
```

time: 819 us -> 112 us (0.14)
  waiting for transfers between devices: 738 us -> 0 us
  Pallas kernels: 0 us -> 105 us
  matrix products: 34.4 us -> 0 us
  local copies, waits for them, and re-layouts: 23.9 us -> 6.7 us
  between operations: 14 us -> 0.01 us
    psum x6 -> x0, waiting for transfers between devices: 403 us -> none  [per_device(): source = source - lax.psum(pending_updates, 'pcol')]
    all_gather x6 -> x0, waiting for transfers between devices: 335 us -> none  [spread_level(): whole_level = lax.all_gather(solved_piece[None], 'prow', axis=0, tiled=True)]
    pallas_call x0 -> x1, Pallas kernels: none -> 105 us  [per_device(): pl.pallas_call(kernel, out_shape=jax.ShapeDtypeStruct(right_sides.shape,...]
    dot_general x28 -> x0, matrix products: 34.4 us -> none  [the longest x12 17.8 us: block_update(): jnp.einsum('kab,kbr->kar', blocks, columns, preferred_element_type=jnp.fl...]
    unnamed x23 -> x11, local copies, waits for them, and re-layouts: 17.8 us -> 6.7 us
  transfers between devices with their start and end apart: 12 -> 0, of which waited for: 12 -> 0; matrix products, arithmetic and copies ran while one was open for 2% -> 0% of each run, Pallas kernels for 0% -> 0%
where the time goes in v1:
time: 112 us
  Pallas kernels  105 us (94%)
  local copies, waits for them, and re-layouts  6.7 us (6%)
    pallas_call x1, Pallas kernels, per_device(): pl.pallas_call(kernel, out_shape=jax.ShapeDtypeStruct(right_sides.shape,...  105 us
    unnamed x11, local copies, waits for them, and re-layouts  6.7 us

profile of v1, /device:TPU:1, one launch (start us, length us, event | category | flops | bytes accessed | tf_op | source)
XLA Modules:
  0.0 111.9 jit_solution(7575051311918877873)
XLA Ops:
  0.0 0.0 copy-start
  0.0 1.9 %copy-done = bf16[6,1,4,256,256]{4,3,2,1,0:T(8,128)(2,1)S(1)} copy-done((bf16[6,1,4,256,256]{4,3,2,1,0:T(8,128)(2,1)S(1)}, bf16[6,1,4,256,256]{4,3,2,1,0:T(8,128)(2,1)}, u32[]{:S(2)}) %copy-start) | copy-done | bytes 3145752
  1.9 0.0 copy-start.1
  1.9 1.0 copy-done.1
  2.9 0.0 copy-start.2
  2.9 1.0 copy-done.2
  4.0 0.0 copy-start.3
  4.0 1.0 copy-done.3
  5.0 0.0 copy-start.4
  5.0 0.9 copy-done.4
  5.9 105.2 %tree_solve.1 = bf16[4,1,256,256]{3,2,1,0:T(8,128)(2,1)S(1)} custom-call(bf16[4,1,256,256]{3,2,1,0:T(8,128)(2,1)S(1)} %copy-done.1, bf16[4,1,256,256]{3,2,1,0:T(8,128)(2,1)S(1)} %copy-done.2, bf16[4,1,256,256]{3,2,1,0:T(8,128)(2,1)S(1)} %copy-done.3, bf16[6,1,4,256,256]{4,3,2,1,0:T(8,128)(2,1)S(1)} %copy-done, bf16[6,1,4,256,256]{4,3,2,1,0:T(8,128)(2,1)} %upper_hbm.1, ...), custom_call_target="tpu_custom_call" | custom-call | tf_op jit(solution)/shard_map/tree_solve/pallas_call | solution.py:496
  111.1 0.8 copy.8
Async XLA Ops:
  0.0 1.9 %copy-start = (bf16[6,1,4,256,256]{4,3,2,1,0:T(8,128)(2,1)S(1)}, bf16[6,1,4,256,256]{4,3,2,1,0:T(8,128)(2,1)}, u32[]{:S(2)}) copy-start(bf16[6,1,4,256,256]{4,3,2,1,0:T(8,128)(2,1)} %lower_hbm.1) | copy-start | bytes 9437188
  1.9 1.0 copy-start.1
  2.9 1.0 copy-start.2
  4.0 1.0 copy-start.3
  5.0 0.9 copy-start.4

commit v2 on v1

--- a/solution.py
+++ b/solution.py
@@ -34,7 +34,7 @@
     rhs, linv, uinv, lower, upper,
     g_all, g_home, home, x0, first_m, part, zsum,
     mov, mov_sib, comb, rs_buf, piece, lact,
-    ucand, ur_buf, upiece, uact0, uact1, uact2,
+    ucand, ur_buf0, ur_buf1, upiece, uact0, uact1, uact2,
     fv, u_src, u21, u32, u31,
     sol, s3, s2, s1, out_buf, out_t,
     load_sem, send_sem, recv_sem,
@@ -99,23 +99,22 @@
         greet(dev(q, other, (z + d) % NZ))
         return 0
 
-    move_src = (q // 2, q % 2)
-
     def greet_move(d, _):
-        greet(dev((q + d) % CHIPS, move_src[1], move_src[0]))
+        greet(dev(8 * core + (q + d) % 8, q % 2, q // 2))
         return 0
 
-    own_move = jnp.logical_and(z == q // 2, core == q % 2)
+    own_move = jnp.logical_and(jnp.logical_and(z == q // 2, core == q % 2), core == q // 8)
+    lax.fori_loop(1, 8, greet_move, 0)
+
+    @pl.when(jnp.logical_not(own_move))
+    def _():
+        greet_move(0, 0)
+
     greet(dev(src_chip, core, src_z))
     greet(dev(src_chip, other, src_z))
     lax.fori_loop(0, NZ, greet_cross, 0)
     lax.fori_loop(1, CHIPS, greet_plane, 0)
     lax.fori_loop(1, NZ, greet_z, 0)
-    lax.fori_loop(1, CHIPS, greet_move, 0)
-
-    @pl.when(jnp.logical_not(own_move))
-    def _():
-        greet(dev(q, move_src[1], move_src[0]))
 
     sent = []
 
@@ -177,32 +176,19 @@
             weight = mask[p, row, 4 * z + k].astype(F32)
             dst[k] = (jnp.dot(linv[ROW_OF[p]], lower[p, k], preferred_element_type=F32) * weight).astype(BF16)
 
-    make_g(0)
-    make_m(2, mov.at[0], True)
-    make_m(0, first_m.at[core, 0], True)
-    pl.semaphore_wait(barrier, 48 - own_move.astype(jnp.int32))
-
-    sem = new_sem("home")
-    mine = pl.ds(pl.multiple_of(core * 128 + z * W, W), W)
-    yours = pl.ds(pl.multiple_of(other * 128 + z * W, W), W)
-    remote(g_all.at[0, mine], home.at[core], sem, dev(home_chip, core, plane))
-    remote(g_all.at[0, yours], home.at[core], sem, dev(home_chip, other, plane))
-    sent.append((sem, home))
+    def compress_upper(n):
+        p = UORD[n]
+        found = jnp.int32(0)
+        at = jnp.int32(0)
+        for k in range(4):
+            bit = mask[p, 4 * z + k, row]
+            found = found + bit
+            at = at + k * bit
+        block = jnp.dot(uinv[core, UROW[n]], upper[p, at], preferred_element_type=F32) * found.astype(F32)
+        ucand[n] = block.astype(BF16)
 
     def move_to_sibling(i):
         to_sibling(("mov", i), mov.at[i, pl.ds(2 * other, 2)], mov_sib.at[i])
-
-    move_to_sibling(0)
-    to_sibling(("m", 0), first_m.at[core, 0], first_m.at[core, 0])
-
-    for h in range(1, LEV):
-        make_g(h)
-    to_sibling("g", g_all.at[:, yours], g_home.at[core])
-    g_home[core] = g_all[:, mine]
-
-    for i in (1, 2):
-        make_m(MOVED[i], mov.at[i], True)
-        move_to_sibling(i)
 
     def combine(i):
         wait_recv(sems[("mov", i)], mov_sib.at[i])
@@ -219,17 +205,6 @@
         lax.fori_loop(1, CHIPS, body, 0)
         rs_buf[i, q] = comb[i, :, pl.ds(pl.multiple_of(q * W, W), W)]
         sent.append((sem, rs_buf.at[i, pl.ds(0, 15)]))
-
-    combine(0)
-
-    wait_recv(sems["home"], home)
-    plane_gather("x0", home, x0, slot)
-
-    for i in (1, 2):
-        make_m(FIRST[i], first_m.at[core, i], True)
-        to_sibling(("m", i), first_m.at[core, i], first_m.at[core, i])
-    combine(1)
-    combine(2)
 
     def spread(i):
         wait_recv(sems[("rs", i)], rs_buf.at[i, pl.ds(0, 15)])
@@ -240,49 +215,41 @@
         sem = new_sem(("lact", i))
         chip = 2 * z + core
 
-        def body(t, _):
-            remote(piece.at[i], lact.at[i, q], sem, dev(chip, (core + t) % 2, (z + t // 2) % NZ))
-            return 0
-
-        lax.fori_loop(1, 16, body, 0)
+        def body(d, _):
+            remote(piece.at[i], lact.at[i, q // 8, q % 8], sem, dev(chip, q // 8, (z + d) % NZ))
+            return 0
+
+        lax.fori_loop(1, NZ, body, 0)
 
         @pl.when(own_move)
         def _():
-            lact[i, q] = piece[i]
+            lact[i, q // 8, q % 8] = piece[i]
 
         @pl.when(jnp.logical_not(own_move))
         def _():
-            remote(piece.at[i], lact.at[i, q], sem, dev(chip, core, z))
+            body(0, 0)
 
         return sem
 
     def wait_moved(sem_ref, i):
         @pl.when(own_move)
         def _():
-            ref = lact.at[i, pl.ds(0, 15)]
+            ref = lact.at[i, 0, pl.ds(0, 7)]
             pltpu.make_async_copy(ref, ref, sem_ref).wait()
 
         @pl.when(jnp.logical_not(own_move))
         def _():
-            ref = lact.at[i]
+            ref = lact.at[i, 0]
             pltpu.make_async_copy(ref, ref, sem_ref).wait()
 
-    spread_sems = [spread(0)]
-
-    loads["uinv"].wait()
-    to_sibling("uinv", uinv.at[core], uinv.at[core])
-    loads["upper"].wait()
-    for n, p in enumerate(UORD):
-        found = jnp.int32(0)
-        at = jnp.int32(0)
-        for k in range(4):
-            bit = mask[p, 4 * z + k, row]
-            found = found + bit
-            at = at + k * bit
-        block = jnp.dot(uinv[core, UROW[n]], upper[p, at], preferred_element_type=F32) * found.astype(F32)
-        ucand[n] = block.astype(BF16)
-
-    plane_wait("x0", x0)
+    spread_sems = {}
+
+    def pass_moved(i):
+        wait_moved(recv_sem.at[spread_sems[i]], i)
+        to_sibling(("ls", i), lact.at[i, core], lact.at[i, core])
+
+    def moved_ready(i):
+        wait_recv(sems[("ls", i)], lact.at[i, 0])
 
     def products(i):
         wait_recv(sems[("m", i)], first_m.at[0, 0])
@@ -293,26 +260,10 @@
                 term = dot_nt(cols, first_m[e, i, k])
                 total = term if total is None else total + term
             part[i, :, e] = total.astype(BF16).reshape(NZ, W, B)
+
+    def send_products(i):
         z_exchange(("z", i), lambda zz: part.at[i, zz], zsum.at[i], z)
         zsum[i, z] = part[i, z]
-
-    products(0)
-    products(1)
-    products(2)
-    spread_sems.append(spread(1))
-    spread_sems.append(spread(2))
-
-    sem = new_sem("ur")
-
-    def ur_body(d, _):
-        zz = (z + d) % NZ
-        rows = pl.ds(pl.multiple_of(zz * 32, 32), 32)
-        remote(ucand.at[:, rows], ur_buf.at[z], sem, dev(q, core, zz))
-        return 0
-
-    lax.fori_loop(1, NZ, ur_body, 0)
-    ur_buf[z] = ucand[:, pl.ds(pl.multiple_of(z * 32, 32), 32)]
-    sent.append((sem, ur_buf.at[pl.ds(0, 7)]))
 
     def z_total(i):
         wait_recv(sems[("z", i)], zsum.at[i, pl.ds(0, 7)])
@@ -321,7 +272,7 @@
             total = total + zsum[i, s].astype(F32)
         return total
 
-    def pushed(i, buf, p):
+    def pushed(buf, p):
         def body(t, carry):
             for j in [t * 8 + u for u in range(8)]:
                 val = buf[j].astype(F32)
@@ -333,26 +284,34 @@
 
     def push(name, level, i, slot_, buf):
         for e in range(2):
-            block = lact[i, :, e].reshape(B, B)
+            block = lact[i, :, :, e].reshape(B, B)
             u_src[slot_, e] = dot_nt(fv[level, e], block).astype(BF16)
         plane_gather(name, u_src.at[slot_], buf, pl.ds(2 * q, 2))
 
-    wait_recv(sems["g"], g_home.at[0])
-    base = z_total(0)
-    for e in range(2):
-        fv[0, e] = g_home[e, 0]
-        fv[1, e] = (g_home[e, 1].astype(F32) - base[e]).astype(BF16)
-    wait_moved(recv_sem.at[spread_sems[0]], 0)
-    push("u21", 1, 0, 0, u21)
-
-    wait_moved(recv_sem.at[spread_sems[2]], 2)
-    push("u31", 1, 2, 1, u31)
-
-    wait_recv(sems["ur"], ur_buf.at[pl.ds(0, 7)])
-    total = ur_buf[0].astype(F32)
-    for s in range(1, NZ):
-        total = total + ur_buf[s].astype(F32)
-    upiece[...] = total.astype(BF16)
+    ur_bufs = (ur_buf0, ur_buf1)
+
+    def reduce_upper(half):
+        sem = new_sem(("ur", half))
+        buf = ur_bufs[half]
+
+        def body(d, _):
+            zz = (z + d) % NZ
+            rows = pl.ds(pl.multiple_of(zz * 32, 32), 32)
+            remote(ucand.at[pl.ds(3 * half, 3), rows], buf.at[z], sem, dev(q, core, zz))
+            return 0
+
+        lax.fori_loop(1, NZ, body, 0)
+        buf[z] = ucand[3 * half:3 * half + 3, pl.ds(pl.multiple_of(z * 32, 32), 32)]
+        sent.append((sem, buf.at[pl.ds(0, 7)]))
+
+    def total_upper(half):
+        buf = ur_bufs[half]
+        wait_recv(sems[("ur", half)], buf.at[pl.ds(0, 7)])
+        total = buf[0].astype(F32)
+        for s in range(1, NZ):
+            total = total + buf[s].astype(F32)
+        upiece[3 * half:3 * half + 3] = total.astype(BF16)
+
     uacts = (uact0, uact1, uact2)
 
     def spread_upper(n):
@@ -375,23 +334,82 @@
     def upper_ready(n):
         wait_recv(sems[("us", n)], uacts[n].at[0])
 
-    for n in range(3):
-        spread_upper(n)
-
+    make_g(0)
+    make_m(2, mov.at[0], True)
+    make_m(0, first_m.at[core, 0], True)
+    for h in range(1, LEV):
+        make_g(h)
+    loads["uinv"].wait()
+    loads["upper"].wait()
+    for n in range(NPAIR):
+        compress_upper(n)
+    pl.semaphore_wait(barrier, 40 - own_move.astype(jnp.int32))
+
+    sem = new_sem("home")
+    mine = pl.ds(pl.multiple_of(core * 128 + z * W, W), W)
+    yours = pl.ds(pl.multiple_of(other * 128 + z * W, W), W)
+    remote(g_all.at[0, mine], home.at[core], sem, dev(home_chip, core, plane))
+    remote(g_all.at[0, yours], home.at[core], sem, dev(home_chip, other, plane))
+    sent.append((sem, home))
+    move_to_sibling(0)
+    to_sibling(("m", 0), first_m.at[core, 0], first_m.at[core, 0])
+    to_sibling("g", g_all.at[:, yours], g_home.at[core])
+    reduce_upper(0)
+    g_home[core] = g_all[:, mine]
+    for i in (1, 2):
+        make_m(MOVED[i], mov.at[i], True)
+        move_to_sibling(i)
+    combine(0)
+
+    wait_recv(sems["home"], home)
+    plane_gather("x0", home, x0, slot)
+    reduce_upper(1)
+    to_sibling("uinv", uinv.at[core], uinv.at[core])
+    for i in (1, 2):
+        make_m(FIRST[i], first_m.at[core, i], True)
+        to_sibling(("m", i), first_m.at[core, i], first_m.at[core, i])
+    spread_sems[0] = spread(0)
+    plane_wait("x0", x0)
+    products(0)
+    send_products(0)
+    combine(1)
+    combine(2)
+    products(1)
+    products(2)
+    total_upper(0)
+    pass_moved(0)
+    wait_recv(sems["g"], g_home.at[0])
+    for e in range(2):
+        fv[0, e] = g_home[e, 0]
+    moved_ready(0)
+    base = z_total(0)
+
+    for e in range(2):
+        fv[1, e] = (g_home[e, 1].astype(F32) - base[e]).astype(BF16)
+    push("u21", 1, 0, 0, u21)
+    spread_sems[1] = spread(1)
+    send_products(1)
+    spread_sems[2] = spread(2)
+    base = g_home[:, 2].astype(F32) - z_total(1)
     plane_wait("u21", u21)
-    low, high = pushed(0, u21, 2)
-    base = g_home[:, 2].astype(F32) - z_total(1)
+    low, high = pushed(u21, 2)
     fv[2, 0] = (base[0] - low).astype(BF16)
     fv[2, 1] = (base[1] - high).astype(BF16)
-    wait_moved(recv_sem.at[spread_sems[1]], 1)
+    pass_moved(1)
+    moved_ready(1)
     push("u32", 2, 1, 2, u32)
-
+    send_products(2)
+    spread_upper(0)
+    pass_moved(2)
+    moved_ready(2)
+    push("u31", 1, 2, 1, u31)
+    total_upper(1)
+    spread_upper(1)
     base = g_home[:, 3].astype(F32) - z_total(2)
+    plane_wait("u32", u32)
+    low, high = pushed(u32, 5)
     plane_wait("u31", u31)
-    low1, high1 = pushed(1, u31, 4)
-    pass_upper(0)
-    plane_wait("u32", u32)
-    low, high = pushed(1, u32, 5)
+    low1, high1 = pushed(u31, 4)
     fv[3, 0] = (base[0] - low1 - low).astype(BF16)
     fv[3, 1] = (base[1] - high1 - high).astype(BF16)
 
@@ -415,9 +433,10 @@
         blocks = [uacts[group][e, :, n - UGROUPS[group][0]].reshape(B, B) for e in range(2)]
         return [dot_nt(chosen[e].astype(BF16), blocks[e]) for e in range(2)]
 
-    def publish(level, buf):
-        if buf is not None:
-            plane_gather(("s", level), sol.at[level], buf, pl.ds(2 * q, 2))
+    def gather_level(level, buf):
+        plane_gather(("s", level), sol.at[level], buf, pl.ds(2 * q, 2))
+
+    def publish(level):
         sem = new_sem(("out", level))
         at = core * 8 + z
 
@@ -446,35 +465,40 @@
 
     for e in range(2):
         sol[3, e] = own_term(3, e).astype(BF16)
-    publish(3, s3)
-    pass_upper(1)
+    gather_level(3, s3)
+    spread_upper(2)
     rest = [own_term(2, e) for e in range(2)]
+    pass_upper(0)
     upper_ready(0)
     plane_wait(("s", 3), s3)
     terms = above(s3, 0)
     for e in range(2):
         sol[2, e] = (rest[e] - terms[e]).astype(BF16)
-    publish(2, s2)
-    pass_upper(2)
+    gather_level(2, s2)
+    publish(3)
+    pass_upper(1)
     upper_ready(1)
     terms = above(s3, 2)
     rest = [own_term(1, e) - terms[e] for e in range(2)]
-    finish(3)
     plane_wait(("s", 2), s2)
     terms = above(s2, 1)
     for e in range(2):
         sol[1, e] = (rest[e] - terms[e]).astype(BF16)
-    publish(1, s1)
+    gather_level(1, s1)
+    publish(2)
+    publish(1)
+    pass_upper(2)
     upper_ready(2)
     terms = above(s3, 5)
     more = above(s2, 4)
     rest = [own_term(0, e) - terms[e] - more[e] for e in range(2)]
-    finish(2)
+    finish(3)
     plane_wait(("s", 1), s1)
     terms = above(s1, 3)
     for e in range(2):
         sol[0, e] = (rest[e] - terms[e]).astype(BF16)
-    publish(0, None)
+    publish(0)
+    finish(2)
     finish(1)
 
     for sem, ref in sent:
@@ -493,10 +517,11 @@
         return pltpu.VMEM(shape, BF16)
 
     anywhere = pl.BlockSpec(memory_space=pl.ANY)
+    hbm = pl.BlockSpec(memory_space=pltpu.HBM)
     return pl.pallas_call(
         kernel,
         out_shape=jax.ShapeDtypeStruct(right_sides.shape, BF16),
-        in_specs=[anywhere] * 5 + [pl.BlockSpec(memory_space=pltpu.SMEM)],
+        in_specs=[hbm] * 5 + [pl.BlockSpec(memory_space=pltpu.SMEM)],
         out_specs=anywhere,
         scratch_shapes=[
             vmem(LEV, B, B),
@@ -516,9 +541,10 @@
             vmem(3, 2, B, B),
             vmem(3, CHIPS, 2, W, B),
             vmem(3, 2, W, B),
-            vmem(3, CHIPS, 2, W, B),
+            vmem(3, 2, 8, 2, W, B),
             vmem(NPAIR, B, B),
-            vmem(NZ, NPAIR, 32, B),
+            vmem(NZ, 3, 32, B),
+            vmem(NZ, 3, 32, B),
             vmem(NPAIR, 32, B),
             vmem(2, NZ, 1, 32, B),
             vmem(2, NZ, 2, 32, B),
@@ -539,7 +565,7 @@
             pltpu.SemaphoreType.DMA((48,)),
         ],
         compiler_params=pltpu.CompilerParams(
-            collective_id=0, has_side_effects=True, vmem_limit_bytes=48 * 2**20
+            collective_id=0, has_side_effects=True, vmem_limit_bytes=63 * 2**20
         ),
         name="tree_solve",
     )(right_sides, lower_diag_inverse, upper_diag_inverse, lower_blocks, upper_blocks, block_mask)

time: 112 us -> 91.7 us (0.82)
  Pallas kernels: 105 us -> 89.6 us
  local copies, waits for them, and re-layouts: 6.7 us -> 1.87 us
    pallas_call x1, Pallas kernels: 105 us -> 89.6 us  [per_device(): pl.pallas_call(kernel, out_shape=jax.ShapeDtypeStruct(right_sides.shape,...]
    unnamed x11 -> x1, local copies, waits for them, and re-layouts: 6.7 us -> 1.87 us
where the time goes in v2:
time: 91.7 us; the launch traced here: 91.5 us
  Pallas kernels  89.6 us (98%)
  local copies, waits for them, and re-layouts  1.87 us (2%)
    pallas_call x1, Pallas kernels, per_device(): pl.pallas_call(kernel, out_shape=jax.ShapeDtypeStruct(right_sides.shape,...  89.6 us
    unnamed x1, local copies, waits for them, and re-layouts  1.87 us

profile of v2, /device:TPU:1, one launch (start us, length us, event | category | flops | bytes accessed | tf_op | source)
XLA Modules:
  0.0 91.5 jit_solution(3363351632229154300)
XLA Ops:
  0.0 89.6 %tree_solve.1 = bf16[4,1,256,256]{3,2,1,0:T(8,128)(2,1)} custom-call(bf16[4,1,256,256]{3,2,1,0:T(8,128)(2,1)} %rhs_hbm.1, bf16[4,1,256,256]{3,2,1,0:T(8,128)(2,1)} %linv_hbm.1, bf16[4,1,256,256]{3,2,1,0:T(8,128)(2,1)} %uinv_hbm.1, bf16[6,1,4,256,256]{4,3,2,1,0:T(8,128)(2,1)} %lower_hbm.1, bf16[6,1,4,256,256]{4,3,2,1,0:T(8,128)(2,1)} %upper_hbm.1, ...), custom_call_target="tpu_custom_call" | custom-call | tf_op jit(solution)/shard_map/tree_solve/pallas_call | solution.py:521
  89.6 1.9 %copy.8 = bf16[4,1,256,256]{3,2,1,0:T(8,128)(2,1)} copy(bf16[4,1,256,256]{3,2,1,0:T(8,128)(2,1)} %tree_solve.1) | data formatting | bytes 1048576

commit v3 on v2

--- a/solution.py
+++ b/solution.py
@@ -22,6 +22,7 @@
 UROW = (2, 1, 1, 0, 0, 0)
 ROW_OF = (1, 2, 2, 3, 3, 3)
 UGROUPS = ((0, 1), (1, 3), (3, 6))
+UHALVES = ((0, 4), (4, 6))
 
 
 def dot_nt(a, b):
@@ -291,26 +292,28 @@
     ur_bufs = (ur_buf0, ur_buf1)
 
     def reduce_upper(half):
+        lo, hi = UHALVES[half]
         sem = new_sem(("ur", half))
         buf = ur_bufs[half]
 
         def body(d, _):
             zz = (z + d) % NZ
             rows = pl.ds(pl.multiple_of(zz * 32, 32), 32)
-            remote(ucand.at[pl.ds(3 * half, 3), rows], buf.at[z], sem, dev(q, core, zz))
+            remote(ucand.at[pl.ds(lo, hi - lo), rows], buf.at[z], sem, dev(q, core, zz))
             return 0
 
         lax.fori_loop(1, NZ, body, 0)
-        buf[z] = ucand[3 * half:3 * half + 3, pl.ds(pl.multiple_of(z * 32, 32), 32)]
+        buf[z] = ucand[lo:hi, pl.ds(pl.multiple_of(z * 32, 32), 32)]
         sent.append((sem, buf.at[pl.ds(0, 7)]))
 
     def total_upper(half):
+        lo, hi = UHALVES[half]
         buf = ur_bufs[half]
         wait_recv(sems[("ur", half)], buf.at[pl.ds(0, 7)])
         total = buf[0].astype(F32)
         for s in range(1, NZ):
             total = total + buf[s].astype(F32)
-        upiece[3 * half:3 * half + 3] = total.astype(BF16)
+        upiece[lo:hi] = total.astype(BF16)
 
     uacts = (uact0, uact1, uact2)
 
@@ -360,10 +363,10 @@
         make_m(MOVED[i], mov.at[i], True)
         move_to_sibling(i)
     combine(0)
+    combine(1)
 
     wait_recv(sems["home"], home)
     plane_gather("x0", home, x0, slot)
-    reduce_upper(1)
     to_sibling("uinv", uinv.at[core], uinv.at[core])
     for i in (1, 2):
         make_m(FIRST[i], first_m.at[core, i], True)
@@ -372,9 +375,10 @@
     plane_wait("x0", x0)
     products(0)
     send_products(0)
-    combine(1)
     combine(2)
     products(1)
+    send_products(1)
+    spread_sems[1] = spread(1)
     products(2)
     total_upper(0)
     pass_moved(0)
@@ -387,9 +391,9 @@
     for e in range(2):
         fv[1, e] = (g_home[e, 1].astype(F32) - base[e]).astype(BF16)
     push("u21", 1, 0, 0, u21)
-    spread_sems[1] = spread(1)
-    send_products(1)
     spread_sems[2] = spread(2)
+    send_products(2)
+    reduce_upper(1)
     base = g_home[:, 2].astype(F32) - z_total(1)
     plane_wait("u21", u21)
     low, high = pushed(u21, 2)
@@ -398,13 +402,11 @@
     pass_moved(1)
     moved_ready(1)
     push("u32", 2, 1, 2, u32)
-    send_products(2)
     spread_upper(0)
+    spread_upper(1)
     pass_moved(2)
     moved_ready(2)
     push("u31", 1, 2, 1, u31)
-    total_upper(1)
-    spread_upper(1)
     base = g_home[:, 3].astype(F32) - z_total(2)
     plane_wait("u32", u32)
     low, high = pushed(u32, 5)
@@ -466,6 +468,7 @@
     for e in range(2):
         sol[3, e] = own_term(3, e).astype(BF16)
     gather_level(3, s3)
+    total_upper(1)
     spread_upper(2)
     rest = [own_term(2, e) for e in range(2)]
     pass_upper(0)
@@ -475,9 +478,9 @@
     for e in range(2):
         sol[2, e] = (rest[e] - terms[e]).astype(BF16)
     gather_level(2, s2)
-    publish(3)
     pass_upper(1)
     upper_ready(1)
+    publish(3)
     terms = above(s3, 2)
     rest = [own_term(1, e) - terms[e] for e in range(2)]
     plane_wait(("s", 2), s2)
@@ -486,18 +489,18 @@
         sol[1, e] = (rest[e] - terms[e]).astype(BF16)
     gather_level(1, s1)
     publish(2)
+    pass_upper(2)
     publish(1)
-    pass_upper(2)
     upper_ready(2)
     terms = above(s3, 5)
     more = above(s2, 4)
     rest = [own_term(0, e) - terms[e] - more[e] for e in range(2)]
-    finish(3)
     plane_wait(("s", 1), s1)
     terms = above(s1, 3)
     for e in range(2):
         sol[0, e] = (rest[e] - terms[e]).astype(BF16)
     publish(0)
+    finish(3)
     finish(2)
     finish(1)
 
@@ -543,8 +546,8 @@
             vmem(3, 2, W, B),
             vmem(3, 2, 8, 2, W, B),
             vmem(NPAIR, B, B),
-            vmem(NZ, 3, 32, B),
-            vmem(NZ, 3, 32, B),
+            vmem(NZ, 4, 32, B),
+            vmem(NZ, 2, 32, B),
             vmem(NPAIR, 32, B),
             vmem(2, NZ, 1, 32, B),
             vmem(2, NZ, 2, 32, B),

time: 91.7 us -> 83.6 us (0.912)
  Pallas kernels: 89.6 us -> 81.6 us
    pallas_call x1, Pallas kernels: 89.6 us -> 81.6 us  [per_device(): pl.pallas_call(kernel, out_shape=jax.ShapeDtypeStruct(right_sides.shape,...]
where the time goes in v3:
time: 83.6 us; the launch traced here: 83.4 us
  Pallas kernels  81.6 us (98%)
  local copies, waits for them, and re-layouts  1.87 us (2%)
    pallas_call x1, Pallas kernels, per_device(): pl.pallas_call(kernel, out_shape=jax.ShapeDtypeStruct(right_sides.shape,...  81.6 us
    unnamed x1, local copies, waits for them, and re-layouts  1.87 us

profile of v3, /device:TPU:1, one launch (start us, length us, event | category | flops | bytes accessed | tf_op | source)
XLA Modules:
  0.0 83.4 jit_solution(4166159439258679106)
XLA Ops:
  0.0 81.6 %tree_solve.1 = bf16[4,1,256,256]{3,2,1,0:T(8,128)(2,1)} custom-call(bf16[4,1,256,256]{3,2,1,0:T(8,128)(2,1)} %rhs_hbm.1, bf16[4,1,256,256]{3,2,1,0:T(8,128)(2,1)} %linv_hbm.1, bf16[4,1,256,256]{3,2,1,0:T(8,128)(2,1)} %uinv_hbm.1, bf16[6,1,4,256,256]{4,3,2,1,0:T(8,128)(2,1)} %lower_hbm.1, bf16[6,1,4,256,256]{4,3,2,1,0:T(8,128)(2,1)} %upper_hbm.1, ...), custom_call_target="tpu_custom_call" | custom-call | tf_op jit(solution)/shard_map/tree_solve/pallas_call | solution.py:524
  81.6 1.9 %copy.8 = bf16[4,1,256,256]{3,2,1,0:T(8,128)(2,1)} copy(bf16[4,1,256,256]{3,2,1,0:T(8,128)(2,1)} %tree_solve.1) | data formatting | bytes 1048576

commit v4 on v3

--- a/solution.py
+++ b/solution.py
@@ -22,7 +22,6 @@
 UROW = (2, 1, 1, 0, 0, 0)
 ROW_OF = (1, 2, 2, 3, 3, 3)
 UGROUPS = ((0, 1), (1, 3), (3, 6))
-UHALVES = ((0, 4), (4, 6))
 
 
 def dot_nt(a, b):
@@ -35,7 +34,7 @@
     rhs, linv, uinv, lower, upper,
     g_all, g_home, home, x0, first_m, part, zsum,
     mov, mov_sib, comb, rs_buf, piece, lact,
-    ucand, ur_buf0, ur_buf1, upiece, uact0, uact1, uact2,
+    ucand, ring_r, ring_l, sum_r, sum_l, upiece, uact0, uact1, uact2,
     fv, u_src, u21, u32, u31,
     sol, s3, s2, s1, out_buf, out_t,
     load_sem, send_sem, recv_sem,
@@ -289,31 +288,32 @@
             u_src[slot_, e] = dot_nt(fv[level, e], block).astype(BF16)
         plane_gather(name, u_src.at[slot_], buf, pl.ds(2 * q, 2))
 
-    ur_bufs = (ur_buf0, ur_buf1)
-
-    def reduce_upper(half):
-        lo, hi = UHALVES[half]
-        sem = new_sem(("ur", half))
-        buf = ur_bufs[half]
-
-        def body(d, _):
-            zz = (z + d) % NZ
-            rows = pl.ds(pl.multiple_of(zz * 32, 32), 32)
-            remote(ucand.at[pl.ds(lo, hi - lo), rows], buf.at[z], sem, dev(q, core, zz))
-            return 0
-
-        lax.fori_loop(1, NZ, body, 0)
-        buf[z] = ucand[lo:hi, pl.ds(pl.multiple_of(z * 32, 32), 32)]
-        sent.append((sem, buf.at[pl.ds(0, 7)]))
-
-    def total_upper(half):
-        lo, hi = UHALVES[half]
-        buf = ur_bufs[half]
-        wait_recv(sems[("ur", half)], buf.at[pl.ds(0, 7)])
-        total = buf[0].astype(F32)
-        for s in range(1, NZ):
-            total = total + buf[s].astype(F32)
-        upiece[lo:hi] = total.astype(BF16)
+    def upper_rows(shift):
+        return pl.ds(pl.multiple_of((z + NZ + shift) % NZ * 32, 32), 32)
+
+    def ring_send(way, n, src):
+        sem = new_sem(("ring", way, n))
+        buf = (ring_r if way > 0 else ring_l).at[n]
+        remote(src, buf, sem, dev(q, core, (z + NZ + way) % NZ))
+        sent.append((sem, buf))
+
+    def ring_start():
+        ring_send(1, 0, ucand.at[:, upper_rows(4)])
+        ring_send(-1, 0, ucand.at[:, upper_rows(-3)])
+
+    def ring_step(n):
+        wait_recv(sems[("ring", 1, n - 1)], ring_r.at[n - 1])
+        sum_r[n - 1] = ring_r[n - 1] + ucand[:, upper_rows(4 - n)]
+        ring_send(1, n, sum_r.at[n - 1])
+        if n < 3:
+            wait_recv(sems[("ring", -1, n - 1)], ring_l.at[n - 1])
+            sum_l[n - 1] = ring_l[n - 1] + ucand[:, upper_rows(n - 3)]
+            ring_send(-1, n, sum_l.at[n - 1])
+
+    def ring_end():
+        wait_recv(sems[("ring", 1, 3)], ring_r.at[3])
+        wait_recv(sems[("ring", -1, 2)], ring_l.at[2])
+        upiece[...] = ring_r[3] + ring_l[2] + ucand[:, upper_rows(0)]
 
     uacts = (uact0, uact1, uact2)
 
@@ -357,7 +357,7 @@
     move_to_sibling(0)
     to_sibling(("m", 0), first_m.at[core, 0], first_m.at[core, 0])
     to_sibling("g", g_all.at[:, yours], g_home.at[core])
-    reduce_upper(0)
+    ring_start()
     g_home[core] = g_all[:, mine]
     for i in (1, 2):
         make_m(MOVED[i], mov.at[i], True)
@@ -368,19 +368,22 @@
     wait_recv(sems["home"], home)
     plane_gather("x0", home, x0, slot)
     to_sibling("uinv", uinv.at[core], uinv.at[core])
+    combine(2)
+    ring_step(1)
     for i in (1, 2):
         make_m(FIRST[i], first_m.at[core, i], True)
         to_sibling(("m", i), first_m.at[core, i], first_m.at[core, i])
     spread_sems[0] = spread(0)
+    ring_step(2)
+    spread_sems[1] = spread(1)
     plane_wait("x0", x0)
     products(0)
     send_products(0)
-    combine(2)
+    ring_step(3)
+    spread_sems[2] = spread(2)
     products(1)
     send_products(1)
-    spread_sems[1] = spread(1)
     products(2)
-    total_upper(0)
     pass_moved(0)
     wait_recv(sems["g"], g_home.at[0])
     for e in range(2):
@@ -391,22 +394,22 @@
     for e in range(2):
         fv[1, e] = (g_home[e, 1].astype(F32) - base[e]).astype(BF16)
     push("u21", 1, 0, 0, u21)
-    spread_sems[2] = spread(2)
     send_products(2)
-    reduce_upper(1)
+    pass_moved(1)
+    pass_moved(2)
+    ring_end()
+    spread_upper(0)
     base = g_home[:, 2].astype(F32) - z_total(1)
     plane_wait("u21", u21)
     low, high = pushed(u21, 2)
     fv[2, 0] = (base[0] - low).astype(BF16)
     fv[2, 1] = (base[1] - high).astype(BF16)
-    pass_moved(1)
     moved_ready(1)
     push("u32", 2, 1, 2, u32)
-    spread_upper(0)
-    spread_upper(1)
-    pass_moved(2)
     moved_ready(2)
     push("u31", 1, 2, 1, u31)
+    for n in (1, 2):
+        spread_upper(n)
     base = g_home[:, 3].astype(F32) - z_total(2)
     plane_wait("u32", u32)
     low, high = pushed(u32, 5)
@@ -468,8 +471,6 @@
     for e in range(2):
         sol[3, e] = own_term(3, e).astype(BF16)
     gather_level(3, s3)
-    total_upper(1)
-    spread_upper(2)
     rest = [own_term(2, e) for e in range(2)]
     pass_upper(0)
     upper_ready(0)
@@ -546,8 +547,10 @@
             vmem(3, 2, W, B),
             vmem(3, 2, 8, 2, W, B),
             vmem(NPAIR, B, B),
-            vmem(NZ, 4, 32, B),
-            vmem(NZ, 2, 32, B),
+            vmem(4, NPAIR, 32, B),
+            vmem(3, NPAIR, 32, B),
+            vmem(3, NPAIR, 32, B),
+            vmem(2, NPAIR, 32, B),
             vmem(NPAIR, 32, B),
             vmem(2, NZ, 1, 32, B),
             vmem(2, NZ, 2, 32, B),

time: 83.6 us -> 81.8 us (0.978)
  Pallas kernels: 81.6 us -> 79.7 us
    pallas_call x1, Pallas kernels: 81.6 us -> 79.7 us  [per_device(): pl.pallas_call(kernel, out_shape=jax.ShapeDtypeStruct(right_sides.shape,...]
where the time goes in v4:
time: 81.8 us; the launch traced here: 81.6 us
  Pallas kernels  79.7 us (97%)
  local copies, waits for them, and re-layouts  1.87 us (2%)
    pallas_call x1, Pallas kernels, per_device(): pl.pallas_call(kernel, out_shape=jax.ShapeDtypeStruct(right_sides.shape,...  79.7 us
    unnamed x1, local copies, waits for them, and re-layouts  1.87 us

profile of v4, /device:TPU:1, one launch (start us, length us, event | category | flops | bytes accessed | tf_op | source)
XLA Modules:
  0.0 81.6 jit_solution(17293159944926042818)
XLA Ops:
  0.0 79.7 %tree_solve.1 = bf16[4,1,256,256]{3,2,1,0:T(8,128)(2,1)} custom-call(bf16[4,1,256,256]{3,2,1,0:T(8,128)(2,1)} %rhs_hbm.1, bf16[4,1,256,256]{3,2,1,0:T(8,128)(2,1)} %linv_hbm.1, bf16[4,1,256,256]{3,2,1,0:T(8,128)(2,1)} %uinv_hbm.1, bf16[6,1,4,256,256]{4,3,2,1,0:T(8,128)(2,1)} %lower_hbm.1, bf16[6,1,4,256,256]{4,3,2,1,0:T(8,128)(2,1)} %upper_hbm.1, ...), custom_call_target="tpu_custom_call" | custom-call | tf_op jit(solution)/shard_map/tree_solve/pallas_call | solution.py:525
  79.7 1.9 %copy.8 = bf16[4,1,256,256]{3,2,1,0:T(8,128)(2,1)} copy(bf16[4,1,256,256]{3,2,1,0:T(8,128)(2,1)} %tree_solve.1) | data formatting | bytes 1048576

commit v5 on v4

--- a/solution.py
+++ b/solution.py
@@ -363,24 +363,22 @@
         make_m(MOVED[i], mov.at[i], True)
         move_to_sibling(i)
     combine(0)
-    combine(1)
 
     wait_recv(sems["home"], home)
     plane_gather("x0", home, x0, slot)
     to_sibling("uinv", uinv.at[core], uinv.at[core])
-    combine(2)
     ring_step(1)
     for i in (1, 2):
         make_m(FIRST[i], first_m.at[core, i], True)
         to_sibling(("m", i), first_m.at[core, i], first_m.at[core, i])
     spread_sems[0] = spread(0)
     ring_step(2)
-    spread_sems[1] = spread(1)
     plane_wait("x0", x0)
     products(0)
     send_products(0)
+    combine(1)
+    combine(2)
     ring_step(3)
-    spread_sems[2] = spread(2)
     products(1)
     send_products(1)
     products(2)
@@ -388,27 +386,28 @@
     wait_recv(sems["g"], g_home.at[0])
     for e in range(2):
         fv[0, e] = g_home[e, 0]
+    spread_sems[1] = spread(1)
     moved_ready(0)
     base = z_total(0)
 
     for e in range(2):
         fv[1, e] = (g_home[e, 1].astype(F32) - base[e]).astype(BF16)
     push("u21", 1, 0, 0, u21)
-    send_products(2)
-    pass_moved(1)
-    pass_moved(2)
+    spread_sems[2] = spread(2)
     ring_end()
-    spread_upper(0)
     base = g_home[:, 2].astype(F32) - z_total(1)
     plane_wait("u21", u21)
     low, high = pushed(u21, 2)
     fv[2, 0] = (base[0] - low).astype(BF16)
     fv[2, 1] = (base[1] - high).astype(BF16)
+    send_products(2)
+    pass_moved(1)
     moved_ready(1)
     push("u32", 2, 1, 2, u32)
+    pass_moved(2)
     moved_ready(2)
     push("u31", 1, 2, 1, u31)
-    for n in (1, 2):
+    for n in range(3):
         spread_upper(n)
     base = g_home[:, 3].astype(F32) - z_total(2)
     plane_wait("u32", u32)
@@ -571,7 +570,7 @@
             pltpu.SemaphoreType.DMA((48,)),
         ],
         compiler_params=pltpu.CompilerParams(
-            collective_id=0, has_side_effects=True, vmem_limit_bytes=63 * 2**20
+            collective_id=0, has_side_effects=True, vmem_limit_bytes=532 * 2**20 // 10
         ),
         name="tree_solve",
     )(right_sides, lower_diag_inverse, upper_diag_inverse, lower_blocks, upper_blocks, block_mask)

time: 81.8 us -> 81.9 us (level)
    unnamed x1 -> x3, local copies, waits for them, and re-layouts: 1.87 us -> 1.69 us
where the time goes in v5:
time: 81.9 us; the launch traced here: 81.8 us
  Pallas kernels  80.1 us (98%)
  local copies, waits for them, and re-layouts  1.69 us (2%)
    pallas_call x1, Pallas kernels, per_device(): pl.pallas_call(kernel, out_shape=jax.ShapeDtypeStruct(right_sides.shape,...  80.1 us
    unnamed x3, local copies, waits for them, and re-layouts  1.69 us

profile of v5, /device:TPU:1, one launch (start us, length us, event | category | flops | bytes accessed | tf_op | source)
XLA Modules:
  0.0 81.8 jit_solution(4675631850254876648)
XLA Ops:
  0.0 0.0 copy-start
  0.0 0.9 %copy-done = s32[6,32,32]{2,1,0:T(8,128)S(1)} copy-done((s32[6,32,32]{2,1,0:T(8,128)S(1)}, s32[6,32,32]{2,1,0:T(8,128)}, u32[]{:S(2)}) %copy-start) | copy-done | bytes 24600
  0.9 80.1 %tree_solve.1 = bf16[4,1,256,256]{3,2,1,0:T(8,128)(2,1)S(1)} custom-call(bf16[4,1,256,256]{3,2,1,0:T(8,128)(2,1)} %rhs_hbm.1, bf16[4,1,256,256]{3,2,1,0:T(8,128)(2,1)} %linv_hbm.1, bf16[4,1,256,256]{3,2,1,0:T(8,128)(2,1)} %uinv_hbm.1, bf16[6,1,4,256,256]{4,3,2,1,0:T(8,128)(2,1)} %lower_hbm.1, bf16[6,1,4,256,256]{4,3,2,1,0:T(8,128)(2,1)} %upper_hbm.1, ...), custom_call_target="tpu_custom_call" | custom-call | tf_op jit(solution)/shard_map/tree_solve/pallas_call | solution.py:524
  81.0 0.8 copy.8
Async XLA Ops:
  0.0 0.9 %copy-start = (s32[6,32,32]{2,1,0:T(8,128)S(1)}, s32[6,32,32]{2,1,0:T(8,128)}, u32[]{:S(2)}) copy-start(s32[6,32,32]{2,1,0:T(8,128)} %mask.1) | copy-start | bytes 73732

commit v6 on v5

--- a/solution.py
+++ b/solution.py
@@ -373,35 +373,35 @@
         to_sibling(("m", i), first_m.at[core, i], first_m.at[core, i])
     spread_sems[0] = spread(0)
     ring_step(2)
+    combine(1)
     plane_wait("x0", x0)
     products(0)
     send_products(0)
-    combine(1)
     combine(2)
     ring_step(3)
     products(1)
     send_products(1)
     products(2)
+    spread_sems[1] = spread(1)
     pass_moved(0)
     wait_recv(sems["g"], g_home.at[0])
     for e in range(2):
         fv[0, e] = g_home[e, 0]
-    spread_sems[1] = spread(1)
+    spread_sems[2] = spread(2)
     moved_ready(0)
     base = z_total(0)
 
     for e in range(2):
         fv[1, e] = (g_home[e, 1].astype(F32) - base[e]).astype(BF16)
     push("u21", 1, 0, 0, u21)
-    spread_sems[2] = spread(2)
     ring_end()
     base = g_home[:, 2].astype(F32) - z_total(1)
+    pass_moved(1)
     plane_wait("u21", u21)
     low, high = pushed(u21, 2)
     fv[2, 0] = (base[0] - low).astype(BF16)
     fv[2, 1] = (base[1] - high).astype(BF16)
     send_products(2)
-    pass_moved(1)
     moved_ready(1)
     push("u32", 2, 1, 2, u32)
     pass_moved(2)

time: 81.9 us -> 82 us (level)
  no operation moved by 1% of the time
where the time goes in v6:
time: 82 us; the launch traced here: 81.9 us
  Pallas kernels  80.2 us (98%)
  local copies, waits for them, and re-layouts  1.69 us (2%)
    pallas_call x1, Pallas kernels, per_device(): pl.pallas_call(kernel, out_shape=jax.ShapeDtypeStruct(right_sides.shape,...  80.2 us
    unnamed x3, local copies, waits for them, and re-layouts  1.69 us

profile of v6, /device:TPU:1, one launch (start us, length us, event | category | flops | bytes accessed | tf_op | source)
XLA Modules:
  0.0 81.9 jit_solution(2590352754724604744)
XLA Ops:
  0.0 0.0 copy-start
  0.0 0.9 %copy-done = s32[6,32,32]{2,1,0:T(8,128)S(1)} copy-done((s32[6,32,32]{2,1,0:T(8,128)S(1)}, s32[6,32,32]{2,1,0:T(8,128)}, u32[]{:S(2)}) %copy-start) | copy-done | bytes 24600
  0.9 80.2 %tree_solve.1 = bf16[4,1,256,256]{3,2,1,0:T(8,128)(2,1)S(1)} custom-call(bf16[4,1,256,256]{3,2,1,0:T(8,128)(2,1)} %rhs_hbm.1, bf16[4,1,256,256]{3,2,1,0:T(8,128)(2,1)} %linv_hbm.1, bf16[4,1,256,256]{3,2,1,0:T(8,128)(2,1)} %uinv_hbm.1, bf16[6,1,4,256,256]{4,3,2,1,0:T(8,128)(2,1)} %lower_hbm.1, bf16[6,1,4,256,256]{4,3,2,1,0:T(8,128)(2,1)} %upper_hbm.1, ...), custom_call_target="tpu_custom_call" | custom-call | tf_op jit(solution)/shard_map/tree_solve/pallas_call | solution.py:524
  81.1 0.8 copy.8
Async XLA Ops:
  0.0 0.9 %copy-start = (s32[6,32,32]{2,1,0:T(8,128)S(1)}, s32[6,32,32]{2,1,0:T(8,128)}, u32[]{:S(2)}) copy-start(s32[6,32,32]{2,1,0:T(8,128)} %mask.1) | copy-start | bytes 73732
